TPU v7x, 512 devices: a whole 4x4x16 slice. The times are simulated.
512 devices in a mesh: seq: 64 (over x, z), tp: 8 (over y, core).
Axes of the slice: x: 4, y: 4, z: 16, core: 2. Of those that a mesh axis runs over, the one named last changes fastest.
Arguments:
- queries: bfloat16 [8192, 4096], P('seq', 'tp'), may hold values from -128 to 128
- rotated_keys: bfloat16 [8192, 1024], P('seq', 'tp'), may hold values from -4.5 to 4.5
- values: bfloat16 [8192, 1024], P('seq', 'tp'), may hold values from -64 to 64
- decay_rates: float32 [64], P('tp'), may hold values from 2e-06 to 0.016
- decay_codes: int32 [8192, 64], P('seq', 'tp'), may hold values from 1 to 8192
- gate_input: bfloat16 [8192, 4096], P('seq', 'tp'), may hold values from -64 to 64
- norm_gain: float32 [4096], P('tp'), may hold values from 0.1 to 1.9
- bc_weight: bfloat16 [4096, 256], P('tp'), may hold values from -0.09375 to 0.09375
Outputs:
- first_pass: float32 [8192, 4096], P('seq', 'tp')
- second_pass: float32 [8192, 4096], P('seq', 'tp')
All inputs are finite; a program needn't handle non-finite values.
Results may differ from a plain program's by a relative error of at most 0.017.
Values may be sent and summed in bfloat16 or wider, within the bound.
A program may use at most 64 MiB of HBM per device.

v0:
```python
import math

import jax
import jax.numpy as jnp
from jax import lax
from jax.sharding import PartitionSpec as P

QUERY_HEADS = 32
KEY_VALUE_HEADS = 8
HEAD_SIZE = 128
SH = 64
SP = 64
NS = 128
WINDOW_LENGTH = 2048
STRETCH = 128


EPSILON = 1e-05


def shifted(block, axis, distance):
    devices = range(lax.axis_size(axis))
    route = [(i - distance, i) for i in devices if i - distance in devices]
    return lax.ppermute(block, axis, route)


def prefix(x, axis, combine, identity):
    peers, index = (lax.axis_size(axis), lax.axis_index(axis))
    everything = jax.tree.map(lambda part: lax.all_gather(part, axis), x)
    start = jax.tree.map(
        lambda part, zero: jnp.broadcast_to(jnp.asarray(zero, part.dtype), part.shape), x, identity
    )

    def step(k, before):
        reached = k < index
        new = combine(before, jax.tree.map(lambda part: part[k], everything))
        return jax.tree.map(lambda a, b: jnp.where(reached, a, b), new, before)

    return lax.fori_loop(0, peers, step, start)


def combine_states(earlier, later):
    return (earlier[0] * later[0], later[0][..., None, None] * earlier[1] + later[1])


def attention(queries, rotated_keys, values):
    tok_rows = queries.shape[0]
    seq_index = lax.axis_index("seq")
    reach = WINDOW_LENGTH // tok_rows
    kv_local = rotated_keys.shape[1] // HEAD_SIZE
    group_length = QUERY_HEADS // KEY_VALUE_HEADS
    paired = jnp.stack([rotated_keys, values], 0)
    moving = paired
    arrived = []
    for counter in range(reach):
        moving = shifted(moving, "seq", 1)
        arrived.append(moving)
    kv_blocks = arrived[::-1]
    window_kv = jnp.concatenate(kv_blocks + [paired], 1)
    grouped = queries.reshape(tok_rows, kv_local, group_length, HEAD_SIZE)
    score_scale = 1.0 / math.sqrt(HEAD_SIZE)
    query_pos = seq_index * tok_rows + jnp.arange(tok_rows, dtype=jnp.int32)
    base_pos = (seq_index - reach) * tok_rows

    def block_scores(key_block):
        key_row_block = lax.dynamic_slice_in_dim(
            window_kv[0], key_block * tok_rows, tok_rows, 0
        ).reshape(tok_rows, kv_local, HEAD_SIZE)
        scores = (
            jnp.einsum("tkgd,skd->kgts", grouped, key_row_block, preferred_element_type=jnp.float32)
            * score_scale
        )
        key_pos = base_pos + key_block * tok_rows + jnp.arange(tok_rows, dtype=jnp.int32)
        allowed = (
            (key_pos[None, :] <= query_pos[:, None])
            & (key_pos[None, :] > query_pos[:, None] - WINDOW_LENGTH)
            & (key_pos[None, :] >= 0)
        )
        return jnp.where(allowed[None, None], scores, -jnp.inf)

    def visit_order(counter):
        return (counter + reach) % (reach + 1)

    def totals(counter, running):
        row_max, row_sum = running
        scores = block_scores(visit_order(counter))
        new_max = jnp.maximum(row_max, jnp.max(scores, axis=3))
        rescale = jnp.exp(row_max - new_max)
        row_sum = row_sum * rescale + jnp.sum(jnp.exp(scores - new_max[..., None]), axis=3)
        return (new_max, row_sum)

    max_init = jnp.full((kv_local, group_length, tok_rows), -jnp.inf, jnp.float32)
    row_max, row_sum = lax.fori_loop(0, reach + 1, totals, (max_init, jnp.zeros_like(max_init)))

    def weighted(counter, accumulated):
        key_block = visit_order(counter)
        scores = block_scores(key_block)
        value_row_block = lax.dynamic_slice_in_dim(
            window_kv[1], key_block * tok_rows, tok_rows, 0
        ).reshape(tok_rows, kv_local, HEAD_SIZE)
        probs = (jnp.exp(scores - row_max[..., None]) / row_sum[..., None]).astype(jnp.bfloat16)
        return accumulated + jnp.einsum(
            "kgts,skd->kgtd", probs, value_row_block, preferred_element_type=jnp.float32
        )

    acc_init = jnp.zeros((kv_local, group_length, tok_rows, HEAD_SIZE), jnp.float32)
    accumulated = lax.fori_loop(0, reach + 1, weighted, acc_init)
    mixed_rows = jnp.transpose(accumulated, (2, 0, 1, 3))
    return mixed_rows.astype(jnp.bfloat16).reshape(tok_rows, kv_local * group_length * HEAD_SIZE)


def core(inputs, decay_rates, decay_codes, gate_input, norm_gain, bc_weight):
    tok_rows = inputs.shape[0]
    head_count = decay_rates.shape[0]
    channels = SH * SP
    as_float = inputs.astype(jnp.float32)
    own_squares = jnp.sum(as_float * as_float, axis=1)
    partial_value = jnp.dot(inputs, bc_weight, preferred_element_type=jnp.float32)
    total_squares = lax.psum(own_squares, "tp")
    spread = jnp.sqrt(total_squares / channels + EPSILON)[:, None]
    projected = lax.psum(partial_value / spread, "tp")
    normed = (as_float / spread).astype(jnp.bfloat16)
    projected = projected.astype(jnp.bfloat16)
    stretch_count = tok_rows // STRETCH
    x_stretches = normed.reshape(stretch_count, STRETCH, head_count, SP)
    b_stretches = projected[:, :NS].reshape(stretch_count, STRETCH, NS)
    c_stretches = projected[:, NS:].reshape(stretch_count, STRETCH, NS)
    summed_codes = jnp.cumsum(
        decay_codes.reshape(stretch_count, STRETCH, head_count), axis=1, dtype=jnp.int32
    )
    log_decay = -decay_rates * summed_codes.astype(jnp.float32)
    decay_by_head = jnp.transpose(log_decay, (0, 2, 1))
    gram_matrix = jnp.einsum(
        "ctn,csn->cts", c_stretches, b_stretches, preferred_element_type=jnp.float32
    )
    lower_mask = jnp.arange(STRETCH)[:, None] >= jnp.arange(STRETCH)[None, :]
    decay_gaps = jnp.where(
        lower_mask, decay_by_head[..., :, None] - decay_by_head[..., None, :], 0.0
    )
    mixing = jnp.where(lower_mask, gram_matrix[:, None] * jnp.exp(decay_gaps), 0.0).astype(
        jnp.bfloat16
    )
    y_local = jnp.einsum("chts,cshp->cthp", mixing, x_stretches, preferred_element_type=jnp.float32)
    tail_decay = jnp.exp(decay_by_head[..., -1:] - decay_by_head)
    b_weighted = (b_stretches.astype(jnp.float32)[:, None] * tail_decay[..., None]).astype(
        jnp.bfloat16
    )
    contrib = jnp.einsum(
        "chsn,cshp->chnp", b_weighted, x_stretches, preferred_element_type=jnp.float32
    )
    stretch_decay = jnp.exp(decay_by_head[..., -1])
    carried_decay = jnp.ones((head_count,), jnp.float32)
    carried_state = jnp.zeros((head_count, NS, SP), jnp.float32)
    carried_state = stretch_decay[0][:, None, None] * carried_state + contrib[0]
    carried_decay = carried_decay * stretch_decay[0]
    unused_decay, entering = prefix(
        (carried_decay, carried_state),
        "seq",
        combine_states,
        (jnp.ones_like(carried_decay), jnp.zeros_like(carried_state)),
    )
    states = [entering]
    stacked = jnp.stack(states, 0)
    c_weighted = c_stretches.astype(jnp.float32)[:, None] * jnp.exp(decay_by_head)[..., None]
    y_carried = jnp.einsum(
        "chtn,chnp->cthp",
        c_weighted,
        stacked,
        precision=lax.Precision.HIGHEST,
        preferred_element_type=jnp.float32,
    )
    outputs = (y_local + y_carried).reshape(tok_rows, head_count * SP)
    gated_out = outputs * jax.nn.silu(gate_input.astype(jnp.float32))
    gate_squares = lax.psum(jnp.sum(gated_out * gated_out, axis=1), "tp")
    out_scale = jnp.sqrt(gate_squares / channels + EPSILON)[:, None]
    return gated_out / out_scale * norm_gain


def on_device(
    queries, rotated_keys, values, decay_rates, decay_codes, gate_input, norm_gain, bc_weight
):
    attended = attention(queries, rotated_keys, values)
    first_pass = core(attended, decay_rates, decay_codes, gate_input, norm_gain, bc_weight)
    pass_input = first_pass.astype(jnp.bfloat16)
    second_pass = core(pass_input, decay_rates, decay_codes, gate_input, norm_gain, bc_weight)
    return (first_pass, second_pass)


def solution(mesh):
    return jax.shard_map(
        on_device,
        mesh=mesh,
        in_specs=(
            P("seq", "tp"),
            P("seq", "tp"),
            P("seq", "tp"),
            P("tp"),
            P("seq", "tp"),
            P("seq", "tp"),
            P("tp"),
            P("tp", None),
        ),
        out_specs=(P("seq", "tp"), P("seq", "tp")),
        check_vma=False,
    )
```

profile of v0, /device:TPU:1, one launch (start us, length us, event | category | flops | bytes accessed | tf_op | source)
XLA Modules:
  0.0 828.5 jit_solution(17543553133491464584)
XLA Ops:
  29.6 4.8 collective-permute-start.4
  35.7 4.9 collective-permute-start.5
  41.9 4.9 collective-permute-start.6
  48.1 5.4 collective-permute-start.7
  54.8 4.7 collective-permute-start.8
  60.8 4.8 collective-permute-start.9
  67.0 4.9 collective-permute-start.10
  73.2 4.9 collective-permute-start.11
  79.7 4.9 collective-permute-start.12
  85.9 4.9 collective-permute-start.13
  92.5 4.8 collective-permute-start.14
  105.2 9.5 %while.62 = (s32[]{:T(128)}, f32[1,4,128]{2,1,0:T(4,128)S(1)}, f32[1,4,128]{2,1,0:T(4,128)S(1)}, s32[]{:T(128)}, bf16[2,2176,128]{2,1,0:T(8,128)(2,1)S(1)}, /*in...) while((s32[]{:T(128)}, f32[1,4,128]{2,1,0:T(4,128)S(1)}, ...), condition=%wide.region_3.4_spmd.clone, body=%wide.region_0.3_spmd.clone.sunk | while | flops 17173644 | bytes 1865240 | solution.py:93
  114.7 12.6 %while.63 = (s32[]{:T(128)}, f32[1,4,128,128]{3,2,1,0:T(8,128)S(1)}, s32[]{:T(128)}, bf16[2,2176,128]{2,1,0:T(8,128)(2,1)S(1)}, bf16[128,1,4,128]{3,0,2,1:T(8,12...) while((s32[]{:T(128)}, ...), condition=%wide.region_5.6_spmd.clone, body=%wide.region_4.5_spmd.clone.sunk | while | flops 34079376 | bytes 2991130 | solution.py:107
  127.5 29.7 %psum.42 = f32[128]{0:T(128)S(1)} all-reduce(f32[128]{0:T(128)S(1)} %multiply_reduce_fusion.2), channel_id=1, replica_groups=mesh['seq'=64,'tp'=8] {'tp'}, use_global_device_ids=true, to_apply=%region_7.8 | all-reduce | flops 128 | bytes 1024 | tf_op jit(solution)/shard_map/psum | solution.py:119
  157.4 22.1 %all-reduce.2 = bf16[128,256]{1,0:T(8,128)(2,1)S(1)} all-reduce(f32[128,256]{1,0:T(8,128)S(1)} %convolution_divide_fusion.1), channel_id=1, replica_groups=mesh['seq'=64,'tp'=8] {'tp'}, use_global_device_ids=true, to_apply=%region_8.9 | all-reduce | flops 32768 | bytes 196608 | tf_op jit(solution)/shard_map/psum | solution.py:121
  181.0 87.1 %all-gather = f32[64,8,1]{1,2,0:T(1,128)S(1)} all-gather(f32[1,8,1]{1,2,0:T(1,128)S(1)} %get-tuple-element.798), channel_id=2, replica_groups=mesh['seq'=64,'tp'=8] {'seq'}, dimensions={0}, use_global_device_ids=true | all-gather | bytes 2080 | tf_op jit(solution)/shard_map/all_gather | solution.py:29
  268.2 121.9 %all-gather.6.cloned.1.call-done = f32[512,128,64]{1,2,0:T(8,128)} async-done(((f32[8,128,64]{1,2,0:T(8,128)}), f32[512,128,64]{1,2,0:T(8,128)}) %all-gather.6.cloned.1.call-update) | async-done | bytes 16777232 | tf_op jit(solution)/shard_map/all_gather | solution.py:29
  390.1 86.9 %while.64 = (s32[]{:T(128)}, f32[8,128,64]{2,1,0:T(8,128)S(1)}, s32[]{:T(128)}, f32[64,8]{1,0:T(8,128)S(1)}, f32[64,8,128,64]{2,3,1,0:T(8,128)}, /*index=5*/s32[]{:T(128)}, s32[]{:T(128)}) while((s32[]{:T(128)}, f32[8,128,64]{2,1,0:T(8,128)S(1)}, s32[]{:T(128)}, f32[64,8]{1,0:T(8,128)S(1)}, f32[64,8,128,64]{2,3,1,0:T(8,128)}, ...), condition=%wide.region_11.12_spmd.clone, body=%wide.region_10.11_spmd.clone.sunk | while | flops 262148 | bytes 1835209 | solution.py:39
  478.7 12.9 %psum.44 = f32[128]{0:T(128)S(1)} all-reduce(f32[128]{0:T(128)S(1)} %multiply_reduce_fusion.1), channel_id=1, replica_groups=mesh['seq'=64,'tp'=8] {'tp'}, use_global_device_ids=true, to_apply=%region_13.14 | all-reduce | flops 128 | bytes 1024 | tf_op jit(solution)/shard_map/psum | solution.py:174
  491.7 14.2 %psum.45 = f32[128]{0:T(128)S(1)} all-reduce(f32[128]{0:T(128)S(1)} %get-tuple-element.781), channel_id=1, replica_groups=mesh['seq'=64,'tp'=8] {'tp'}, use_global_device_ids=true, to_apply=%region_15.16 | all-reduce | flops 128 | bytes 1024 | tf_op jit(solution)/shard_map/psum | solution.py:119
  506.2 22.1 %all-reduce.3 = bf16[128,256]{1,0:T(8,128)(2,1)S(1)} all-reduce(f32[128,256]{1,0:T(8,128)S(1)} %convolution_divide_fusion), channel_id=1, replica_groups=mesh['seq'=64,'tp'=8] {'tp'}, use_global_device_ids=true, to_apply=%region_16.17 | all-reduce | flops 32768 | bytes 196608 | tf_op jit(solution)/shard_map/psum | solution.py:121
  530.4 188.9 %all-gather.8.cloned.1.call-done = f32[512,128,64]{1,2,0:T(8,128)} async-done(((f32[8,128,64]{1,2,0:T(8,128)}), f32[512,128,64]{1,2,0:T(8,128)}) %all-gather.8.cloned.1.call-update) | async-done | bytes 16777232 | tf_op jit(solution)/shard_map/all_gather | solution.py:29
  719.3 86.9 %while.65 = (s32[]{:T(128)}, f32[8,128,64]{2,1,0:T(8,128)S(1)}, s32[]{:T(128)}, f32[64,8]{1,0:T(8,128)S(1)}, f32[64,8,128,64]{2,3,1,0:T(8,128)}, /*index=5*/s32[]{:T(128)}, s32[]{:T(128)}) while((s32[]{:T(128)}, f32[8,128,64]{2,1,0:T(8,128)S(1)}, s32[]{:T(128)}, f32[64,8]{1,0:T(8,128)S(1)}, f32[64,8,128,64]{2,3,1,0:T(8,128)}, ...), condition=%wide.region_18.19_spmd.clone, body=%wide.region_17.18_spmd.clone.sunk | while | flops 262148 | bytes 1835209 | solution.py:39
  807.8 12.9 %psum.47 = f32[128]{0:T(128)S(1)} all-reduce(f32[128]{0:T(128)S(1)} %multiply_reduce_fusion), channel_id=1, replica_groups=mesh['seq'=64,'tp'=8] {'tp'}, use_global_device_ids=true, to_apply=%region_20.21 | all-reduce | flops 128 | bytes 1024 | tf_op jit(solution)/shard_map/psum | solution.py:174
  (883 shorter events, 239.7 us)
Async XLA Ops:
  7.2 150.0 %copy-start = (bf16[512,256]{1,0:T(8,128)(2,1)S(1)}, bf16[512,256]{1,0:T(8,128)(2,1)}, u32[]{:S(2)}) copy-start(bf16[512,256]{1,0:T(8,128)(2,1)} %param.23) | copy-start | bytes 786436
  7.2 383.0 %all-gather.6.cloned.1.call-start = ((), (), s32[]{:S(2)}) async-start(), calls=%async_computation | async-start | bytes 17039360 | tf_op jit(solution)/shard_map/all_gather | solution.py:29
  8.0 5.7 collective-permute-start
  13.7 5.0 collective-permute-start.1
  18.7 5.4 collective-permute-start.2
  24.2 5.4 collective-permute-start.3
  29.6 6.1 collective-permute-start.4
  35.7 6.2 collective-permute-start.5
  41.9 6.2 collective-permute-start.6
  48.1 6.7 collective-permute-start.7
  54.8 6.0 collective-permute-start.8
  60.8 6.1 collective-permute-start.9
  67.0 6.2 collective-permute-start.10
  73.2 6.5 collective-permute-start.11
  79.7 6.2 collective-permute-start.12
  85.9 6.6 collective-permute-start.13
  92.5 6.1 collective-permute-start.14
  98.6 5.9 collective-permute-start.15
  104.4 0.8 copy-start.2
  104.4 0.8 copy-start.3
  157.4 23.4 %copy-start.1 = (bf16[128,512]{1,0:T(8,128)(2,1)S(1)}, bf16[128,512]{1,0:T(8,128)(2,1)}, u32[]{:S(2)}) copy-start(bf16[128,512]{1,0:T(8,128)(2,1)} %param.21) | copy-start | bytes 393220
  180.7 538.6 %all-gather.8.cloned.1.call-start = ((), (), s32[]{:S(2)}) async-start(), calls=%async_computation.1 | async-start | bytes 17039360 | tf_op jit(solution)/shard_map/all_gather | solution.py:29
  478.2 13.4 %copy-start.4 = (f32[512]{0:T(512)S(1)}, f32[512]{0:T(512)}, u32[]{:S(2)}) copy-start(f32[512]{0:T(512)} %param.22) | copy-start | bytes 6148
Sparse Core Ops, SparseCore 0:
  180.8 209.3 all-gather.5
  529.6 189.7 all-gather.7
where the time goes:
time: 833 us; the launch traced here: 829 us
  waiting for transfers between devices  330 us (40%)
  blocking collectives  201 us (24%)
  local copies, waits for them, and re-layouts  158 us (19%)
  starting transfers between devices  74.3 us (9%)
  other arithmetic  24.5 us (3%)
  matrix products  17.2 us (2%)
  between operations  14.5 us (2%)
  loops' own time  8.83 us (1%)
    all_gather x2, waiting for transfers between devices, prefix(): everything = jax.tree.map(lambda part: lax.all_gather(part, axis), x)  311 us
    dynamic_slice x256, local copies, waits for them, and re-layouts, step(): new = combine(before, jax.tree.map(lambda part: part[k], everything))  150 us
    all_gather x1, blocking collectives, prefix(): everything = jax.tree.map(lambda part: lax.all_gather(part, axis), x)  87.1 us
    ppermute x16, starting transfers between devices, shifted(): return lax.ppermute(block, axis, route)  74.3 us
    psum x2, blocking collectives, core(): projected = lax.psum(partial_value / spread, 'tp')  44.2 us
    psum x2, blocking collectives, core(): total_squares = lax.psum(own_squares, 'tp')  43.8 us
    psum x2, blocking collectives, core(): gate_squares = lax.psum(jnp.sum(gated_out * gated_out, axis=1), 'tp')  25.7 us
    ppermute x16, waiting for transfers between devices, shifted(): return lax.ppermute(block, axis, route)  19.1 us
  transfers between devices with their start and end apart: 18, of which 16 were waited for; matrix products, arithmetic and copies ran while one was open for 1% of the time, Pallas kernels for 0%

commit v1 on v0

v1 whole, which is shorter than its diff:
```python
import functools
import math

import jax
import jax.numpy as jnp
from jax import lax
from jax.experimental import pallas as pl
from jax.experimental.pallas import tpu as pltpu
from jax.sharding import PartitionSpec as P

HEADS = 4
HS = 128
NH = 8
PAIRS = NH // 2
ROWS = 128
REACH = 16
NZ = 16
NX = 4
NT = 8
CHANNELS = 4096
COLS = 512
EPS = 1e-5
SLICE = 32
BF = jnp.bfloat16
F32 = jnp.float32
MESH = pl.DeviceIdType.MESH
NEG = -1e30
FIRST = (3, 13, 1, 15, 16)
RELAY = {3: (6, 4, 2), 13: (10, 14, 12), 6: (8, 7, 5), 10: (9, 11)}
NEAR = (1, 2, 3, 13, 15)


def dot(a, b, ca=1, cb=0):
    return lax.dot_general(a, b, (((ca,), (cb,)), ((), ())), preferred_element_type=F32)


def split(a):
    hi = a.astype(BF).astype(F32)
    return hi, a - hi


def rows4(a):
    return jnp.concatenate([a] * 4, 0)


def pack4(a, b, lane):
    ah, al = split(a)
    bh, bl = split(b)
    return jnp.where(lane < 64, jnp.where(lane < 32, ah, al), jnp.where(lane < 96, bh, bl))


def unpack4(v):
    return v[:, 0:1] + v[:, 32:33], v[:, 64:65] + v[:, 96:97]


def kernel(
    q_hbm, k_hbm, v_hbm, rates, codes_hbm, gate_hbm, gain_hbm, w_hbm,
    out1, out2,
    q_s, k_s, v_s, codes_s, gate_s, gain_s, w_s,
    sc_s, m_s, l_s, decay_s, tail_s, expell_s, silu_s,
    dexp_s, dz_s, dp_s,
    x_s, gated_s, y_s,
    pay_s, rs_s, agsrc_s, ag_s,
    cb_s, e1_s, pre_s, tsrc_s, t_s, e3src_s, st_s,
    gsrc_s, g_s,
    in_sem,
    kv_ss, kv_rs, d_ss, d_rs,
    rs_ss, rs_rs, ag_ss, ag_rs,
    e1_ss, e1_rs, t_ss, t_rs, e3_ss, e3_rs,
    g_ss, g_rs,
):
    s = lax.axis_index("seq")
    t = lax.axis_index("tp")
    x = lax.div(s, NZ)
    z = lax.rem(s, NZ)

    def zpeer(j):
        o = lax.rem(z + j, NZ)
        return o, (x * NZ + o, t)

    def xpeer(j):
        o = lax.rem(x + j, NX)
        return o, (o * NZ + z, t)

    def tpeer(j):
        o = lax.rem(t + j, NT)
        return o, (s, o)

    def remote(src, dst, ss, rs, dev):
        return pltpu.make_async_remote_copy(
            src_ref=src, dst_ref=dst, send_sem=ss, recv_sem=rs, device_id=dev, device_id_type=MESH
        )

    def each(n, body):
        def step(j, c):
            body(j)
            return c

        lax.fori_loop(1, n, step, 0)

    loads = [
        pltpu.make_async_copy(src, dst, in_sem.at[i])
        for i, (src, dst) in enumerate(
            (
                (codes_hbm, codes_s),
                (q_hbm, q_s),
                (k_hbm, k_s.at[0]),
                (v_hbm, v_s.at[0]),
                (gate_hbm, gate_s),
                (gain_hbm, gain_s.at[0]),
                (w_hbm, w_s),
            )
        )
    ]
    for c in loads:
        c.start()

    barrier = pltpu.get_barrier_semaphore()

    def greet(dev):
        pl.semaphore_signal(barrier, inc=1, device_id=dev, device_id_type=MESH)

    def block_device(k):
        return (lax.rem(s + (k + NX * NZ), NX * NZ), t)

    for k in NEAR:
        greet(block_device(k))
        greet(block_device(-k))
    each(NX, lambda j: greet(xpeer(j)[1]))
    each(NZ, lambda j: greet(zpeer(j)[1]))
    each(NT, lambda j: greet(tpeer(j)[1]))

    row = lax.broadcasted_iota(jnp.int32, (ROWS, ROWS), 0)
    col = lax.broadcasted_iota(jnp.int32, (ROWS, ROWS), 1)
    lane1 = lax.broadcasted_iota(jnp.int32, (1, 128), 1)
    lower = row >= col
    upper = jnp.where(row <= col, 1.0, 0.0).astype(BF)
    loads[0].wait()
    codes = codes_s[...]
    code_hi = lax.shift_right_logical(codes, 7).astype(F32).astype(BF)
    code_lo = (codes & 127).astype(F32).astype(BF)
    cum_rows = dot(code_hi, upper) * 128.0 + dot(code_lo, upper)
    cum = jnp.transpose(jnp.concatenate([cum_rows, jnp.zeros((128 - NH, ROWS), F32)], 0))
    for hp in range(PAIRS):
        tails, ells, ends = [], [], []
        for h in (2 * hp, 2 * hp + 1):
            rate = -rates[h]
            ell = cum[:, h : h + 1] * rate
            ell_row = cum_rows[h : h + 1, :] * rate
            end = ell[ROWS - 1 :, :]
            gap = jnp.where(lower, ell - ell_row, 0.0)
            decay_s[h] = jnp.where(lower, jnp.exp(gap), 0.0)
            tails.append(jnp.exp(end - ell))
            ells.append(jnp.exp(ell))
            ends.append(jnp.exp(end))
        cs = slice(hp * 128, hp * 128 + 128)
        tail_s[:, cs] = jnp.where(col < 64, tails[0], tails[1])
        expell_s[:, cs] = jnp.where(col < 64, ells[0], ells[1])
        dexp_s[hp] = jnp.broadcast_to(jnp.where(lane1 < 64, ends[0], ends[1]), (8, 128))

    loads[1].wait()
    loads[2].wait()
    loads[3].wait()
    scale = math.log2(math.e) / math.sqrt(HS)
    diff = col - row
    own_k = k_s[0]
    for h in range(HEADS):
        qh = q_s[:, h * HS : (h + 1) * HS]
        sc = jnp.where(lower, dot(qh, own_k, 1, 1), NEG)
        m = jnp.max(sc, axis=1, keepdims=True)
        m_s[h] = jnp.broadcast_to(m, (ROWS, HS))
        l_s[h] = jnp.exp2((sc - m) * scale)
        sc_s[0, h] = sc

    loads[4].wait()
    g = gate_s[...].astype(F32)
    silu_s[...] = g / (1.0 + jnp.exp(-g))

    pl.semaphore_wait(barrier, 2 * len(NEAR) + (NX - 1) + (NZ - 1) + (NT - 1))

    def hop(i, a, b):
        buf = (k_s, v_s)[i]
        return remote(buf.at[a], buf.at[b], kv_ss.at[i, b], kv_rs.at[i, b], block_device(b - a))

    def arrived(i, b):
        hop(i, b - 1, b).wait_recv()

    for i in range(2):
        for b in FIRST:
            hop(i, 0, b).start()

    def d_send(j):
        o, dev = zpeer(j)
        remote(dexp_s.at[lax.div(o, 4)], dz_s.at[z], d_ss.at[o], d_rs.at[z], dev).start()

    each(NZ, d_send)
    dz_s[z] = dexp_s[lax.div(z, 4)]

    def d_wait(j):
        o, dev = zpeer(j)
        remote(dexp_s.at[0], dz_s.at[o], d_ss.at[o], d_rs.at[o], dev).wait_recv()

    def decay_products():
        each(NZ, d_wait)
        running = jnp.ones((8, 128), F32)
        for zz in range(NZ):
            dp_s[zz] = running
            running = running * dz_s[zz]
        for p in range(2):
            tsrc_s[p, SLICE:] = running

    def relay(a):
        for i in range(2):
            arrived(i, a)
            for b in RELAY[a]:
                hop(i, a, b).start()

    def come(*slots):
        for b in slots:
            arrived(0, b)
            arrived(1, b)

    def attend(a, b):
        big = jnp.int32(1 << 20)

        def limit(k):
            return jnp.where(s >= k, jnp.int32((k - REACH) * ROWS), big)

        keys = jnp.concatenate([k_s[a], k_s[b]], 0)
        ok = jnp.concatenate([diff > limit(a), diff > limit(b)], 1)
        for h in range(HEADS):
            qh = q_s[:, h * HS : (h + 1) * HS]
            sc = jnp.where(ok, dot(qh, keys, 1, 1), NEG)
            old = m_s[h]
            m = jnp.maximum(old, jnp.max(sc, axis=1, keepdims=True))
            alpha = jnp.exp2((old - m) * scale)
            mm = jnp.concatenate([m, m], 1)
            p = jnp.exp2((sc - mm) * scale)
            m_s[h] = m
            l_s[h] = l_s[h] * alpha + (p[:, :HS] + p[:, HS:])
            sc_s[a, h] = sc[:, :HS]
            sc_s[b, h] = sc[:, HS:]

    relay(3)
    relay(13)
    decay_products()
    come(1, 15)
    attend(1, 15)
    attend(3, 13)
    relay(6)
    relay(10)
    come(16, 2, 4, 14, 12)
    attend(2, 16)
    attend(4, 14)
    attend(6, 12)
    come(5)
    attend(5, 10)
    come(7, 11)
    attend(7, 11)
    come(8, 9)
    attend(8, 9)
    for h in range(HEADS):
        m = m_s[h]
        inv = 1.0 / jnp.sum(l_s[h], axis=1, keepdims=True)
        mixed = jnp.zeros((ROWS, HS), F32)
        for a in range(0, REACH, 2):
            parts = [(jnp.exp2((sc_s[k, h] - m) * scale) * inv).astype(BF) for k in (a, a + 1)]
            mixed = mixed + dot(jnp.concatenate(parts, 1), v_s[a : a + 2].reshape(2 * ROWS, HS))
        last = (jnp.exp2((sc_s[REACH, h] - m) * scale) * inv).astype(BF)
        mixed = mixed + dot(last, v_s[REACH])
        x_s[:, h * HS : (h + 1) * HS] = mixed.astype(BF)

    loads[5].wait()
    loads[6].wait()

    def kv_done():
        for i in range(2):
            for b in FIRST:
                hop(i, 0, b).wait_send()
            for a, bs in RELAY.items():
                for b in bs:
                    hop(i, a, b).wait_send()

    def d_done(j):
        o, dev = zpeer(j)
        remote(dexp_s.at[0], dz_s.at[z], d_ss.at[o], d_rs.at[z], dev).wait_send()

    def z_done(p):
        def body(j):
            o, dev = zpeer(j)
            remote(cb_s.at[p, o], e1_s.at[p, z], e1_ss.at[p, o], e1_rs.at[p, z], dev).wait_send()
            remote(e3src_s.at[p, o], st_s.at[p, z], e3_ss.at[p, o], e3_rs.at[p, z], dev).wait_send()

        return body

    def x_done(p):
        def body(j):
            o, dev = xpeer(j)
            remote(tsrc_s.at[p], t_s.at[p, x], t_ss.at[p, o], t_rs.at[p, x], dev).wait_send()

        return body

    def t_done(p):
        def body(j):
            o, dev = tpeer(j)
            remote(pay_s.at[p, o], rs_s.at[p, t], rs_ss.at[p, o], rs_rs.at[p, t], dev).wait_send()
            remote(agsrc_s.at[p], ag_s.at[p, t], ag_ss.at[p, o], ag_rs.at[p, t], dev).wait_send()

        return body

    def g_done(j):
        o, dev = tpeer(j)
        remote(gsrc_s, g_s.at[t], g_ss.at[o], g_rs.at[t], dev).wait_send()

    lane16 = lax.broadcasted_iota(jnp.int32, (16, 128), 1)

    for p in range(2):
        if p == 0:
            xb = x_s[...]
            xf = xb.astype(F32)
            s1 = s2 = jnp.sum(xf * xf, axis=1, keepdims=True)
        else:
            gv = gated_s[...]
            s1 = jnp.sum(gv * gv, axis=1, keepdims=True)
            gg = gv * gain_s[...]
            s2 = jnp.sum(gg * gg, axis=1, keepdims=True)
            xb = gg.astype(BF)
        partial = jnp.concatenate([dot(xb, w_s[...]), pack4(s1, s2, col)], 1)
        pay_s[p] = partial.reshape(NT, 16, 384)

        def rs_send(j, p=p):
            o, dev = tpeer(j)
            remote(pay_s.at[p, o], rs_s.at[p, t], rs_ss.at[p, o], rs_rs.at[p, t], dev).start()

        def rs_wait(j, p=p):
            o, dev = tpeer(j)
            remote(pay_s.at[p, o], rs_s.at[p, o], rs_ss.at[p, o], rs_rs.at[p, o], dev).wait_recv()

        each(NT, rs_send)
        rs_s[p, t] = pay_s[p, t]
        each(NT, rs_wait)
        tot = jnp.sum(rs_s[p], axis=0)
        q1, q2 = unpack4(tot[:, 256:])
        if p == 0:
            scale1 = jnp.ones_like(q1)
        else:
            scale1 = jnp.sqrt(q1 * (1.0 / CHANNELS) + EPS)
        spread = jnp.sqrt(q2 / (scale1 * scale1) * (1.0 / CHANNELS) + EPS)
        proj = tot[:, :256] / (scale1 * spread)
        own = jnp.concatenate([proj, pack4(scale1, spread, lane16)], 1).astype(BF)
        agsrc_s[p] = own
        ag_s[p, t] = own

        def ag_send(j, p=p):
            o, dev = tpeer(j)
            remote(agsrc_s.at[p], ag_s.at[p, t], ag_ss.at[p, o], ag_rs.at[p, t], dev).start()

        def ag_wait(j, p=p):
            o, dev = tpeer(j)
            remote(agsrc_s.at[p], ag_s.at[p, o], ag_ss.at[p, o], ag_rs.at[p, o], dev).wait_recv()

        each(NT, ag_send)
        each(NT, ag_wait)
        agv = ag_s[p].reshape(ROWS, 384)
        b_in = agv[:, :128]
        c_out = agv[:, 128:256]
        scale1, spread = unpack4(agv[:, 256:].astype(F32))
        if p == 1:
            f1 = gated_s[...] * (1.0 / scale1) * gain_s[...]
            out1[...] = f1
            xf = f1.astype(BF).astype(F32)
        xn = (xf * (1.0 / spread)).astype(BF)

        b_rows = jnp.transpose(b_in.astype(F32)).astype(BF)
        contrib = dot(b_rows, (xn.astype(F32) * tail_s[...]).astype(BF)).astype(BF)
        for o in range(NZ):
            hp, nq = o // 4, o % 4
            cb_s[p, o] = contrib[nq * SLICE : (nq + 1) * SLICE, hp * 128 : (hp + 1) * 128]

        def e1_send(j, p=p):
            o, dev = zpeer(j)
            remote(cb_s.at[p, o], e1_s.at[p, z], e1_ss.at[p, o], e1_rs.at[p, z], dev).start()

        def e1_wait(j, p=p):
            o, dev = zpeer(j)
            remote(cb_s.at[p, o], e1_s.at[p, o], e1_ss.at[p, o], e1_rs.at[p, o], dev).wait_recv()

        each(NZ, e1_send)
        e1_s[p, z] = cb_s[p, z]

        gram = dot(c_out, b_rows)
        for hp in range(PAIRS):
            cs = slice(hp * 128, hp * 128 + 128)
            mix = jnp.concatenate([gram * decay_s[2 * hp], gram * decay_s[2 * hp + 1]], 1).astype(BF)
            xp = xn[:, cs]
            zero = jnp.zeros_like(xp)
            both = jnp.concatenate([jnp.where(col < 64, xp, zero), jnp.where(col < 64, zero, xp)], 0)
            y_s[:, cs] = dot(mix, both)

        if p == 0:
            kv_done()
            each(NZ, d_done)
        else:
            each(NZ, z_done(0))
            each(NX, x_done(0))
            each(NT, t_done(0))
        each(NZ, e1_wait)
        state = jnp.zeros((SLICE, 128), F32)
        for zz in range(NZ):
            pre_s[zz] = state
            state = rows4(dz_s[zz]) * state + e1_s[p, zz].astype(F32)
        tsrc_s[p, :SLICE] = state
        t_s[p, x] = tsrc_s[p]

        def t_send(j, p=p):
            o, dev = xpeer(j)
            remote(tsrc_s.at[p], t_s.at[p, x], t_ss.at[p, o], t_rs.at[p, x], dev).start()

        def t_wait(j, p=p):
            o, dev = xpeer(j)
            remote(tsrc_s.at[p], t_s.at[p, o], t_ss.at[p, o], t_rs.at[p, o], dev).wait_recv()

        each(NX, t_send)
        each(NX, t_wait)
        before = jnp.zeros((SLICE, 128), F32)
        for xx in range(NX - 1):
            before = jnp.where(xx < x, rows4(t_s[p, xx, SLICE:]) * before + t_s[p, xx, :SLICE], before)
        for zz in range(NZ):
            e3src_s[p, zz] = (pre_s[zz] + rows4(dp_s[zz]) * before).astype(BF)

        def e3_send(j, p=p):
            o, dev = zpeer(j)
            remote(e3src_s.at[p, o], st_s.at[p, z], e3_ss.at[p, o], e3_rs.at[p, z], dev).start()

        def e3_wait(j, p=p):
            o, dev = zpeer(j)
            remote(e3src_s.at[p, o], st_s.at[p, o], e3_ss.at[p, o], e3_rs.at[p, o], dev).wait_recv()

        each(NZ, e3_send)
        st_s[p, z] = e3src_s[p, z]
        each(NZ, e3_wait)
        for hp in range(PAIRS):
            cs = slice(hp * 128, hp * 128 + 128)
            st = st_s[p, 4 * hp : 4 * hp + 4].reshape(128, 128)
            y = y_s[:, cs] + dot(c_out, st) * expell_s[:, cs]
            gated_s[:, cs] = y * silu_s[:, cs]

    gv = gated_s[...]
    hi, lo = split(gv * gv)
    ones8 = jnp.ones((8, COLS), BF)
    mine = dot(ones8, hi.astype(BF), 1, 1) + dot(ones8, lo.astype(BF), 1, 1)
    gsrc_s[...] = mine
    g_s[t] = mine

    def g_send(j):
        o, dev = tpeer(j)
        remote(gsrc_s, g_s.at[t], g_ss.at[o], g_rs.at[t], dev).start()

    def g_wait(j):
        o, dev = tpeer(j)
        remote(gsrc_s, g_s.at[o], g_ss.at[o], g_rs.at[o], dev).wait_recv()

    each(NT, g_send)
    each(NZ, z_done(1))
    each(NX, x_done(1))
    each(NT, t_done(1))
    each(NT, g_wait)
    total = jnp.sum(g_s[...], axis=0)[0:1, :]
    inv = lax.rsqrt(total * (1.0 / CHANNELS) + EPS)
    inv = jnp.transpose(jnp.broadcast_to(inv, (128, 128)))
    for hp in range(PAIRS):
        cs = slice(hp * 128, hp * 128 + 128)
        out2[:, cs] = gated_s[:, cs] * inv * gain_s[:, cs]
    each(NT, g_done)


def on_device(
    queries, rotated_keys, values, decay_rates, decay_codes, gate_input, norm_gain, bc_weight
):
    vm = pltpu.VMEM
    dma = pltpu.SemaphoreType.DMA
    anyspace = pl.BlockSpec(memory_space=pl.ANY)
    block = vm((ROWS, COLS), F32)
    scratch = [
        vm((ROWS, COLS), BF),
        vm((REACH + 1, ROWS, HS), BF),
        vm((REACH + 1, ROWS, HS), BF),
        vm((NH, ROWS), jnp.int32),
        vm((ROWS, COLS), BF),
        vm((1, COLS), F32),
        vm((COLS, 256), BF),
        vm((REACH + 1, HEADS, ROWS, HS), F32),
        vm((HEADS, ROWS, HS), F32),
        vm((HEADS, ROWS, HS), F32),
        vm((NH, ROWS, ROWS), F32),
        vm((ROWS, COLS), F32),
        vm((ROWS, COLS), F32),
        vm((ROWS, COLS), F32),
        vm((PAIRS, 8, 128), F32),
        vm((NZ, 8, 128), F32),
        vm((NZ, 8, 128), F32),
        vm((ROWS, COLS), BF),
        vm((ROWS, COLS), F32),
        vm((ROWS, COLS), F32),
        vm((2, NT, 16, 384), F32),
        vm((2, NT, 16, 384), F32),
        vm((2, 16, 384), BF),
        vm((2, NT, 16, 384), BF),
        vm((2, NZ, SLICE, 128), BF),
        vm((2, NZ, SLICE, 128), BF),
        vm((NZ, SLICE, 128), F32),
        vm((2, SLICE + 8, 128), F32),
        vm((2, NX, SLICE + 8, 128), F32),
        vm((2, NZ, SLICE, 128), BF),
        vm((2, NZ, SLICE, 128), BF),
        vm((8, 128), F32),
        vm((NT, 8, 128), F32),
        dma((7,)),
        dma((2, REACH + 1)), dma((2, REACH + 1)),
        dma((NZ,)), dma((NZ,)),
        dma((2, NT)), dma((2, NT)), dma((2, NT)), dma((2, NT)),
        dma((2, NZ)), dma((2, NZ)), dma((2, NX)), dma((2, NX)), dma((2, NZ)), dma((2, NZ)),
        dma((NT,)), dma((NT,)),
    ]
    return pl.pallas_call(
        kernel,
        out_shape=(block, block),
        in_specs=[anyspace] * 3 + [pl.BlockSpec(memory_space=pltpu.SMEM)] + [anyspace] * 4,
        out_specs=(pl.BlockSpec(memory_space=vm),) * 2,
        scratch_shapes=scratch,
        compiler_params=pltpu.CompilerParams(
            collective_id=0, has_side_effects=True, vmem_limit_bytes=60 << 20
        ),
    )(queries, rotated_keys, values, decay_rates, decay_codes.T, gate_input, norm_gain, bc_weight)


def solution(mesh):
    return jax.shard_map(
        on_device,
        mesh=mesh,
        in_specs=(
            P("seq", "tp"),
            P("seq", "tp"),
            P("seq", "tp"),
            P("tp"),
            P("seq", "tp"),
            P("seq", "tp"),
            P("tp"),
            P("tp", None),
        ),
        out_specs=(P("seq", "tp"), P("seq", "tp")),
        check_vma=False,
    )
```

time: 833 us -> 122 us (0.15)
  waiting for transfers between devices: 330 us -> 0 us
  blocking collectives: 201 us -> 0 us
  local copies, waits for them, and re-layouts: 158 us -> 1.41 us
  Pallas kernels: 0 us -> 119 us
  starting transfers between devices: 74.3 us -> 0 us
  other arithmetic: 24.5 us -> 0 us
  matrix products: 17.2 us -> 0 us
  between operations: 14.5 us -> 0.64 us
  loops' own time: 8.83 us -> 0 us
    all_gather x2 -> x0, waiting for transfers between devices: 311 us -> none  [prefix(): everything = jax.tree.map(lambda part: lax.all_gather(part, axis), x)]
    dynamic_slice x256 -> x0, local copies, waits for them, and re-layouts: 150 us -> none  [step(): new = combine(before, jax.tree.map(lambda part: part[k], everything))]
    pallas_call x0 -> x1, Pallas kernels: none -> 119 us  [on_device(): pl.pallas_call(kernel, out_shape=(block, block), in_specs=[anyspace] * 3...]
    psum x6 -> x0, blocking collectives: 114 us -> none  [the longest x2 44.2 us: core(): projected = lax.psum(partial_value / spread, 'tp')]
    all_gather x1 -> x0, blocking collectives: 87.1 us -> none  [prefix(): everything = jax.tree.map(lambda part: lax.all_gather(part, axis), x)]
    ppermute x16 -> x0, starting transfers between devices: 74.3 us -> none  [shifted(): return lax.ppermute(block, axis, route)]
    ppermute x16 -> x0, waiting for transfers between devices: 19.1 us -> none  [shifted(): return lax.ppermute(block, axis, route)]
    dot_general x44 -> x0, matrix products: 17.2 us -> none  [the longest x17 7.78 us: weighted(): jnp.einsum('kgts,skd->kgtd', probs, value_row_block, preferred_element_ty...]
  transfers between devices with their start and end apart: 18 -> 0, of which waited for: 16 -> 0; matrix products, arithmetic and copies ran while one was open for 1% -> 0% of each run, Pallas kernels for 0% -> 0%
where the time goes in v1:
time: 122 us; the launch traced here: 121 us
  Pallas kernels  119 us (98%)
  local copies, waits for them, and re-layouts  1.41 us (1%)
    pallas_call x1, Pallas kernels, on_device(): pl.pallas_call(kernel, out_shape=(block, block), in_specs=[anyspace] * 3...  119 us

profile of v1, /device:TPU:1, one launch (start us, length us, event | category | flops | bytes accessed | tf_op | source)
XLA Modules:
  0.0 121.5 jit_solution(10771631610128996924)
XLA Ops:
  0.6 119.4 %shard_map.95 = (f32[128,512]{1,0:T(8,128)S(1)}, f32[128,512]{1,0:T(8,128)S(1)}) custom-call(bf16[128,512]{1,0:T(8,128)(2,1)} %q_hbm.1, bf16[128,128]{1,0:T(8,128)(2,1)} %k_hbm.1, bf16[128,128]{1,0:T(8,128)(2,1)} %v_hbm.1, f32[8]{0:T(128)} %rates.1, s32[8,128]{1,0:T(8,128)} %bitcast.1, bf16[128,512]{1,0:T(8,128)(2,1)} %gate_hbm.1, f32[512]{0:T(512)} %gain_hbm.1, ...), custom_call_target="tpu_custom_call" | custom-call | tf_op jit(solution)/shard_map/pallas_call | solution.py:525
  120.0 0.7 copy.12
  120.8 0.7 copy.13

commit v2 on v1

v2 whole, which is shorter than its diff:
```python
import functools
import math

import jax
import jax.numpy as jnp
from jax import lax
from jax.experimental import pallas as pl
from jax.experimental.pallas import tpu as pltpu
from jax.sharding import PartitionSpec as P

HEADS = 4
HS = 128
NH = 8
PAIRS = NH // 2
ROWS = 128
REACH = 16
NZ = 16
NX = 4
NT = 8
NY = 4
HALF = 64
CHANNELS = 4096
COLS = 512
EPS = 1e-5
SLICE = 16
BF = jnp.bfloat16
F32 = jnp.float32
MESH = pl.DeviceIdType.MESH
NEG = -1e30
FIRST = (3, 13, 1, 15, 16)
RELAY = {3: (6, 4, 2), 13: (10, 14, 12), 6: (8, 7, 5), 10: (9, 11)}
NEAR = (1, 2, 3, 13, 15)


def dot(a, b, ca=1, cb=0):
    return lax.dot_general(a, b, (((ca,), (cb,)), ((), ())), preferred_element_type=F32)


def split(a):
    hi = a.astype(BF).astype(F32)
    return hi, a - hi


def pack4(a, b, lane):
    ah, al = split(a)
    bh, bl = split(b)
    return jnp.where(lane < 64, jnp.where(lane < 32, ah, al), jnp.where(lane < 96, bh, bl))


def unpack4(v):
    return v[:, 0:1] + v[:, 32:33], v[:, 64:65] + v[:, 96:97]


def kernel(
    q_hbm, k_hbm, v_hbm, rates, codes_hbm, gate_hbm, gain_hbm, w_hbm,
    out1, out2,
    q_s, k_s, v_s, codes_s, gate_s, gain_s, w_s,
    sc_s, m_s, l_s, decay_s, tail_s, expell_s, silu_s,
    dexp_s, dz_s, dp_s,
    x_s, gated_s, y_s,
    pay_s, pr_s, ysrc_s, rs_s, ag_s,
    cb_s, e1_s, pre_s, tsrc_s, t_s, e3src_s, st_s,
    gsrc_s, g_s,
    in_sem,
    kv_ss, kv_rs, d_ss, d_rs,
    pair_ss, pair_rs, rs_ss, rs_rs, ag_ss, ag_rs,
    e1_ss, e1_rs, t_ss, t_rs, e3_ss, e3_rs,
    g_ss, g_rs,
):
    s = lax.axis_index("seq")
    t = lax.axis_index("tp")
    x = lax.div(s, NZ)
    z = lax.rem(s, NZ)
    chip = lax.div(t, 2)
    core = lax.rem(t, 2)
    partner = (s, t + 1 - 2 * core)

    def zpeer(j):
        o = lax.rem(z + j, NZ)
        return o, (x * NZ + o, t)

    def xpeer(j):
        o = lax.rem(x + j, NX)
        return o, (o * NZ + z, t)

    def tpeer(j):
        o = lax.rem(t + j, NT)
        return o, (s, o)

    def ypeer(j):
        o = lax.rem(chip + j, NY)
        return o, (s, 2 * o + core)

    def remote(src, dst, ss, rs, dev):
        return pltpu.make_async_remote_copy(
            src_ref=src, dst_ref=dst, send_sem=ss, recv_sem=rs, device_id=dev, device_id_type=MESH
        )

    def all_in(ref, sem):
        remote(ref, ref, sem, sem, partner).wait_recv()

    def all_out(ref, sem):
        remote(ref, ref, sem, sem, partner).wait_send()

    def each(n, body):
        def step(j, c):
            body(j)
            return c

        lax.fori_loop(1, n, step, 0)

    barrier = pltpu.get_barrier_semaphore()

    def greet(dev):
        pl.semaphore_signal(barrier, inc=1, device_id=dev, device_id_type=MESH)

    def block_device(k):
        return (lax.rem(s + (k + NX * NZ), NX * NZ), t)

    for k in NEAR:
        greet(block_device(k))
        greet(block_device(-k))
    each(NX, lambda j: greet(xpeer(j)[1]))
    each(NZ, lambda j: greet(zpeer(j)[1]))
    each(NT, lambda j: greet(tpeer(j)[1]))

    loads = [
        pltpu.make_async_copy(src, dst, in_sem.at[i])
        for i, (src, dst) in enumerate(
            (
                (k_hbm, k_s.at[0]),
                (v_hbm, v_s.at[0]),
                (codes_hbm, codes_s),
                (q_hbm, q_s),
                (gate_hbm, gate_s),
                (gain_hbm, gain_s.at[0]),
                (w_hbm, w_s),
            )
        )
    ]
    for c in loads:
        c.start()

    pl.semaphore_wait(barrier, 2 * len(NEAR) + (NX - 1) + (NZ - 1) + (NT - 1))

    def hop(i, a, b):
        buf = (k_s, v_s)[i]
        return remote(buf.at[a], buf.at[b], kv_ss.at[i, b], kv_rs.at[i, b], block_device(b - a))

    def arrived(i, b):
        hop(i, b - 1, b).wait_recv()

    loads[0].wait()
    loads[1].wait()
    for group in (FIRST[:2], FIRST[2:]):
        for i in range(2):
            for b in group:
                hop(i, 0, b).start()

    row = lax.broadcasted_iota(jnp.int32, (ROWS, ROWS), 0)
    col = lax.broadcasted_iota(jnp.int32, (ROWS, ROWS), 1)
    lane1 = lax.broadcasted_iota(jnp.int32, (1, 128), 1)
    lower = row >= col
    upper = jnp.where(row <= col, 1.0, 0.0).astype(BF)
    loads[2].wait()
    codes = codes_s[...]
    code_hi = lax.shift_right_logical(codes, 7).astype(F32).astype(BF)
    code_lo = (codes & 127).astype(F32).astype(BF)
    cum_rows = dot(code_hi, upper) * 128.0 + dot(code_lo, upper)
    cum = jnp.transpose(jnp.concatenate([cum_rows, jnp.zeros((128 - NH, ROWS), F32)], 0))
    for hp in range(PAIRS):
        ells, ends = [], []
        for h in (2 * hp, 2 * hp + 1):
            rate = -rates[h]
            ell = cum[:, h : h + 1] * rate
            ell_row = cum_rows[h : h + 1, :] * rate
            end = ell[ROWS - 1 :, :]
            gap = jnp.where(lower, ell - ell_row, 0.0)
            decay_s[h] = jnp.where(lower, jnp.exp(gap), 0.0)
            tail_s[h : h + 1, :] = jnp.exp(end - ell_row)
            ells.append(jnp.exp(ell))
            ends.append(jnp.exp(end))
        cs = slice(hp * 128, hp * 128 + 128)
        expell_s[:, cs] = jnp.where(col < 64, ells[0], ells[1])
        dexp_s[hp % 2, hp // 2 : hp // 2 + 1, :] = jnp.where(lane1 < 64, ends[0], ends[1])

    def d_send(j):
        o, dev = zpeer(j)
        remote(dexp_s.at[lax.div(o, 8)], dz_s.at[z], d_ss, d_rs, dev).start()

    each(NZ, d_send)
    dz_s[z] = dexp_s[lax.div(z, 8)]

    loads[3].wait()
    scale = math.log2(math.e) / math.sqrt(HS)
    diff = col - row
    own_k = k_s[0]
    for h in range(HEADS):
        qh = q_s[:, h * HS : (h + 1) * HS]
        sc = jnp.where(lower, dot(qh, own_k, 1, 1), NEG)
        m = jnp.max(sc, axis=1, keepdims=True)
        m_s[h] = jnp.broadcast_to(m, (ROWS, HS))
        l_s[h] = jnp.exp2((sc - m) * scale)
        sc_s[0, h] = sc

    loads[4].wait()
    g = gate_s[...].astype(F32)
    silu_s[...] = g / (1.0 + jnp.exp(-g))

    def decay_products():
        all_in(dz_s.at[pl.ds(0, NZ - 1)], d_rs)
        running = jnp.ones((2, 128), F32)
        for zz in range(NZ):
            dp_s[zz] = running
            running = running * dz_s[zz]
        for p in range(2):
            for half in range(2):
                tsrc_s[2 * p + half, SLICE:] = jnp.broadcast_to(running[half : half + 1], (8, 128))

    def relay(a, b):
        for i in range(2):
            for k in (a, b):
                arrived(i, k)
                hop(i, k, RELAY[k][0]).start()
        for n in (1, 2):
            for k in (a, b):
                for i in range(2):
                    for to in RELAY[k][n : n + 1]:
                        hop(i, k, to).start()

    def come(*slots):
        for b in slots:
            arrived(0, b)
            arrived(1, b)

    def attend(a, b):
        big = jnp.int32(1 << 20)

        def limit(k):
            return jnp.where(s >= k, jnp.int32((k - REACH) * ROWS), big)

        keys = jnp.concatenate([k_s[a], k_s[b]], 0)
        ok = jnp.concatenate([diff > limit(a), diff > limit(b)], 1)
        for h in range(HEADS):
            qh = q_s[:, h * HS : (h + 1) * HS]
            sc = jnp.where(ok, dot(qh, keys, 1, 1), NEG)
            old = m_s[h]
            m = jnp.maximum(old, jnp.max(sc, axis=1, keepdims=True))
            alpha = jnp.exp2((old - m) * scale)
            mm = jnp.concatenate([m, m], 1)
            p = jnp.exp2((sc - mm) * scale)
            m_s[h] = m
            l_s[h] = l_s[h] * alpha + (p[:, :HS] + p[:, HS:])
            sc_s[a, h] = sc[:, :HS]
            sc_s[b, h] = sc[:, HS:]

    relay(3, 13)
    come(1, 15)
    attend(1, 15)
    attend(3, 13)
    relay(6, 10)
    come(16, 2, 4, 14, 12)
    attend(2, 16)
    attend(4, 14)
    attend(6, 12)
    come(5)
    attend(5, 10)
    come(7, 11)
    attend(7, 11)
    come(8, 9)
    attend(8, 9)
    decay_products()
    for h in range(HEADS):
        m = m_s[h]
        inv = 1.0 / jnp.sum(l_s[h], axis=1, keepdims=True)
        mixed = jnp.zeros((ROWS, HS), F32)
        for a in range(0, REACH, 2):
            parts = [(jnp.exp2((sc_s[k, h] - m) * scale) * inv).astype(BF) for k in (a, a + 1)]
            mixed = mixed + dot(jnp.concatenate(parts, 1), v_s[a : a + 2].reshape(2 * ROWS, HS))
        last = (jnp.exp2((sc_s[REACH, h] - m) * scale) * inv).astype(BF)
        mixed = mixed + dot(last, v_s[REACH])
        x_s[:, h * HS : (h + 1) * HS] = mixed.astype(BF)

    loads[5].wait()
    loads[6].wait()

    def kv_done():
        for i in range(2):
            for b in FIRST:
                hop(i, 0, b).wait_send()
            for a, bs in RELAY.items():
                for b in bs:
                    hop(i, a, b).wait_send()

    def pass_done(p):
        pair_copy(p).wait_send()
        share_copy(p, core).wait_send()
        all_out(rs_s.at[p, pl.ds(0, NY - 1)], rs_ss.at[p])
        for q in (2 * p, 2 * p + 1):
            all_out(e1_s.at[q, pl.ds(0, NZ - 1)], e1_ss.at[q])
            all_out(t_s.at[q, pl.ds(0, NX - 1)], t_ss.at[q])
            all_out(st_s.at[q, pl.ds(0, NZ - 1)], e3_ss.at[q])

    lane_half = lax.broadcasted_iota(jnp.int32, (HALF, 128), 1)

    def e1_copy(q, to, slot):
        o, dev = to
        return remote(cb_s.at[q, o], e1_s.at[q, slot], e1_ss.at[q], e1_rs.at[q], dev)

    def t_copy(q, to, slot):
        o, dev = to
        return remote(tsrc_s.at[q], t_s.at[q, slot], t_ss.at[q], t_rs.at[q], dev)

    def e3_copy(q, to, slot):
        o, dev = to
        return remote(e3src_s.at[q, o], st_s.at[q, slot], e3_ss.at[q], e3_rs.at[q], dev)

    def pair_copy(p):
        return remote(pay_s.at[p, 1 - core], pr_s.at[p], pair_ss.at[p], pair_rs.at[p], partner)

    def y_copy(p, o, dev, slot):
        return remote(ysrc_s.at[p], rs_s.at[p, slot], rs_ss.at[p], rs_rs.at[p], dev)

    def share_copy(p, half):
        return remote(ag_s.at[p, half], ag_s.at[p, half], ag_ss.at[p], ag_rs.at[p], partner)


    for p in range(2):
        if p == 0:
            xb = x_s[...]
            xf = xb.astype(F32)
            s1 = s2 = jnp.sum(xf * xf, axis=1, keepdims=True)
        else:
            gv = gated_s[...]
            s1 = jnp.sum(gv * gv, axis=1, keepdims=True)
            gg = gv * gain_s[...]
            s2 = jnp.sum(gg * gg, axis=1, keepdims=True)
            xb = gg.astype(BF)
        partial = jnp.concatenate([dot(xb, w_s[...]), pack4(s1, s2, col)], 1)
        pay_s[p] = partial.reshape(2, HALF, 384)
        pair = pair_copy(p)
        pair.start()
        pair.wait_recv()
        both = pay_s[p, core] + pr_s[p]
        q1, q2 = unpack4(both[:, 256:])
        mine = jnp.concatenate([both[:, :256], pack4(q1, q2, lane_half)], 1).astype(BF)
        ysrc_s[p] = mine
        rs_s[p, chip] = mine
        each(NY, lambda j, p=p: y_copy(p, ypeer(j)[0], ypeer(j)[1], chip).start())
        all_in(rs_s.at[p, pl.ds(0, NY - 1)], rs_rs.at[p])
        tot = jnp.sum(rs_s[p].astype(F32), axis=0)
        q1, q2 = unpack4(tot[:, 256:])
        if p == 0:
            scale1 = jnp.ones_like(q1)
        else:
            scale1 = jnp.sqrt(q1 * (1.0 / CHANNELS) + EPS)
        spread = jnp.sqrt(q2 / (scale1 * scale1) * (1.0 / CHANNELS) + EPS)
        proj = tot[:, :256] / (scale1 * spread)
        ag_s[p, core] = jnp.concatenate([proj, pack4(scale1, spread, lane_half)], 1).astype(BF)
        share_copy(p, core).start()
        share_copy(p, 1 - core).wait_recv()
        agv = ag_s[p].reshape(ROWS, 384)
        b_in = agv[:, :128]
        c_out = agv[:, 128:256]
        scale1, spread = unpack4(agv[:, 256:].astype(F32))
        if p == 1:
            f1 = gated_s[...] * (1.0 / scale1) * gain_s[...]
            out1[...] = f1
            xf = f1.astype(BF).astype(F32)
        xn = (xf * (1.0 / spread)).astype(BF)

        b_wide = jnp.transpose(b_in.astype(F32))
        b_rows = b_wide.astype(BF)
        for half in range(2):
            for hp in (2 * half, 2 * half + 1):
                xp = xn[:, hp * 128 : hp * 128 + 128]
                one, two = [
                    dot((b_wide * tail_s[h : h + 1, :]).astype(BF), xp) for h in (2 * hp, 2 * hp + 1)
                ]
                contrib = jnp.where(col < 64, one, two).astype(BF)
                for nq in range(8):
                    cb_s[2 * p + half, 8 * (hp % 2) + nq] = contrib[nq * SLICE : (nq + 1) * SLICE]
            each(NZ, lambda j, q=2 * p + half: e1_copy(q, zpeer(j), z).start())
            e1_s[2 * p + half, z] = cb_s[2 * p + half, z]

        gram = dot(c_out, b_rows)
        for hp in range(PAIRS):
            cs = slice(hp * 128, hp * 128 + 128)
            mix = jnp.concatenate([gram * decay_s[2 * hp], gram * decay_s[2 * hp + 1]], 1).astype(BF)
            xp = xn[:, cs]
            zero = jnp.zeros_like(xp)
            both = jnp.concatenate([jnp.where(col < 64, xp, zero), jnp.where(col < 64, zero, xp)], 0)
            y_s[:, cs] = dot(mix, both)

        if p == 0:
            kv_done()
            all_out(dz_s.at[pl.ds(0, NZ - 1)], d_ss)
        else:
            pass_done(0)
        for half in range(2):
            q = 2 * p + half
            all_in(e1_s.at[q, pl.ds(0, NZ - 1)], e1_rs.at[q])
            state = jnp.zeros((SLICE, 128), F32)
            for zz in range(NZ):
                pre_s[half, zz] = state
                state = dz_s[zz, half : half + 1, :] * state + e1_s[q, zz].astype(F32)
            tsrc_s[q, :SLICE] = state
            t_s[q, x] = tsrc_s[q]
            each(NX, lambda j, q=q: t_copy(q, xpeer(j), x).start())
        for half in range(2):
            q = 2 * p + half
            all_in(t_s.at[q, pl.ds(0, NX - 1)], t_rs.at[q])
            before = jnp.zeros((SLICE, 128), F32)
            for xx in range(NX - 1):
                decay = t_s[q, xx, SLICE : SLICE + 1]
                before = jnp.where(xx < x, decay * before + t_s[q, xx, :SLICE], before)
            for zz in range(NZ):
                e3src_s[q, zz] = (pre_s[half, zz] + dp_s[zz, half : half + 1, :] * before).astype(BF)
            each(NZ, lambda j, q=q: e3_copy(q, zpeer(j), z).start())
            st_s[q, z] = e3src_s[q, z]
        for half in range(2):
            q = 2 * p + half
            all_in(st_s.at[q, pl.ds(0, NZ - 1)], e3_rs.at[q])
            for hp in (2 * half, 2 * half + 1):
                cs = slice(hp * 128, hp * 128 + 128)
                st = st_s[q, 8 * (hp % 2) : 8 * (hp % 2) + 8].reshape(128, 128)
                y = y_s[:, cs] + dot(c_out, st) * expell_s[:, cs]
                gated_s[:, cs] = y * silu_s[:, cs]

    gv = gated_s[...]
    hi, lo = split(gv * gv)
    ones8 = jnp.ones((8, COLS), BF)
    mine = dot(ones8, hi.astype(BF), 1, 1) + dot(ones8, lo.astype(BF), 1, 1)
    gsrc_s[...] = mine
    g_s[t] = mine

    def g_send(j):
        o, dev = tpeer(j)
        remote(gsrc_s, g_s.at[t], g_ss, g_rs, dev).start()

    each(NT, g_send)
    pass_done(1)
    all_in(g_s.at[pl.ds(0, NT - 1)], g_rs)
    total = jnp.sum(g_s[...], axis=0)[0:1, :]
    inv = lax.rsqrt(total * (1.0 / CHANNELS) + EPS)
    inv = jnp.transpose(jnp.broadcast_to(inv, (128, 128)))
    for hp in range(PAIRS):
        cs = slice(hp * 128, hp * 128 + 128)
        out2[:, cs] = gated_s[:, cs] * inv * gain_s[:, cs]
    all_out(g_s.at[pl.ds(0, NT - 1)], g_ss)


def on_device(
    queries, rotated_keys, values, decay_rates, decay_codes, gate_input, norm_gain, bc_weight
):
    vm = pltpu.VMEM
    dma = pltpu.SemaphoreType.DMA
    anyspace = pl.BlockSpec(memory_space=pl.ANY)
    block = vm((ROWS, COLS), F32)
    scratch = [
        vm((ROWS, COLS), BF),
        vm((REACH + 1, ROWS, HS), BF),
        vm((REACH + 1, ROWS, HS), BF),
        vm((NH, ROWS), jnp.int32),
        vm((ROWS, COLS), BF),
        vm((1, COLS), F32),
        vm((COLS, 256), BF),
        vm((REACH + 1, HEADS, ROWS, HS), F32),
        vm((HEADS, ROWS, HS), F32),
        vm((HEADS, ROWS, HS), F32),
        vm((NH, ROWS, ROWS), F32),
        vm((NH, ROWS), F32),
        vm((ROWS, COLS), F32),
        vm((ROWS, COLS), F32),
        vm((2, 2, 128), F32),
        vm((NZ, 2, 128), F32),
        vm((NZ, 2, 128), F32),
        vm((ROWS, COLS), BF),
        vm((ROWS, COLS), F32),
        vm((ROWS, COLS), F32),
        vm((2, 2, HALF, 384), F32),
        vm((2, HALF, 384), F32),
        vm((2, HALF, 384), BF),
        vm((2, NY, HALF, 384), BF),
        vm((2, 2, HALF, 384), BF),
        vm((4, NZ, SLICE, 128), BF),
        vm((4, NZ, SLICE, 128), BF),
        vm((2, NZ, SLICE, 128), F32),
        vm((4, SLICE + 8, 128), F32),
        vm((4, NX, SLICE + 8, 128), F32),
        vm((4, NZ, SLICE, 128), BF),
        vm((4, NZ, SLICE, 128), BF),
        vm((8, 128), F32),
        vm((NT, 8, 128), F32),
        dma((7,)),
        dma((2, REACH + 1)), dma((2, REACH + 1)),
        dma, dma,
        dma((2,)), dma((2,)), dma((2,)), dma((2,)), dma((2,)), dma((2,)),
        dma((4,)), dma((4,)), dma((4,)), dma((4,)), dma((4,)), dma((4,)),
        dma, dma,
    ]
    return pl.pallas_call(
        kernel,
        out_shape=(block, block),
        in_specs=[anyspace] * 3 + [pl.BlockSpec(memory_space=pltpu.SMEM)] + [anyspace] * 4,
        out_specs=(pl.BlockSpec(memory_space=vm),) * 2,
        scratch_shapes=scratch,
        compiler_params=pltpu.CompilerParams(
            collective_id=0, has_side_effects=True, vmem_limit_bytes=60 << 20
        ),
    )(queries, rotated_keys, values, decay_rates, decay_codes.T, gate_input, norm_gain, bc_weight)


def solution(mesh):
    return jax.shard_map(
        on_device,
        mesh=mesh,
        in_specs=(
            P("seq", "tp"),
            P("seq", "tp"),
            P("seq", "tp"),
            P("tp"),
            P("seq", "tp"),
            P("seq", "tp"),
            P("tp"),
            P("tp", None),
        ),
        out_specs=(P("seq", "tp"), P("seq", "tp")),
        check_vma=False,
    )
```

time: 122 us -> 111 us (0.910)
  Pallas kernels: 119 us -> 109 us
    pallas_call x1, Pallas kernels: 119 us -> 109 us  [on_device(): pl.pallas_call(kernel, out_shape=(block, block), in_specs=[anyspace] * 3...]
where the time goes in v2:
time: 111 us
  Pallas kernels  109 us (98%)
  local copies, waits for them, and re-layouts  1.41 us (1%)
    pallas_call x1, Pallas kernels, on_device(): pl.pallas_call(kernel, out_shape=(block, block), in_specs=[anyspace] * 3...  109 us

profile of v2, /device:TPU:1, one launch (start us, length us, event | category | flops | bytes accessed | tf_op | source)
XLA Modules:
  0.0 111.2 jit_solution(5384993967915291127)
XLA Ops:
  0.6 109.1 %shard_map.95 = (f32[128,512]{1,0:T(8,128)S(1)}, f32[128,512]{1,0:T(8,128)S(1)}) custom-call(bf16[128,512]{1,0:T(8,128)(2,1)} %q_hbm.1, bf16[128,128]{1,0:T(8,128)(2,1)} %k_hbm.1, bf16[128,128]{1,0:T(8,128)(2,1)} %v_hbm.1, f32[8]{0:T(128)} %rates.1, s32[8,128]{1,0:T(8,128)} %bitcast.1, bf16[128,512]{1,0:T(8,128)(2,1)} %gate_hbm.1, f32[512]{0:T(512)} %gain_hbm.1, ...), custom_call_target="tpu_custom_call" | custom-call | tf_op jit(solution)/shard_map/pallas_call | solution.py:502
  109.8 0.7 copy.12
  110.5 0.7 copy.13

commit v3 on v2

--- a/solution.py
+++ b/solution.py
@@ -21,6 +21,7 @@
 HALF = 64
 CHANNELS = 4096
 COLS = 512
+NS = 128
 EPS = 1e-5
 SLICE = 16
 BF = jnp.bfloat16
@@ -58,12 +59,12 @@
     sc_s, m_s, l_s, decay_s, tail_s, expell_s, silu_s,
     dexp_s, dz_s, dp_s,
     x_s, gated_s, y_s,
-    pay_s, pr_s, ysrc_s, rs_s, ag_s,
+    pay_s, pr_s, ysrc_s, rs_s, ag_s, csrc_s, cs_s, agc_s,
     cb_s, e1_s, pre_s, tsrc_s, t_s, e3src_s, st_s,
     gsrc_s, g_s,
     in_sem,
     kv_ss, kv_rs, d_ss, d_rs,
-    pair_ss, pair_rs, rs_ss, rs_rs, ag_ss, ag_rs,
+    pair_ss, pair_rs, rs_ss, rs_rs, ag_ss, ag_rs, cs_ss, cs_rs, agc_ss, agc_rs,
     e1_ss, e1_rs, t_ss, t_rs, e3_ss, e3_rs,
     g_ss, g_rs,
 ):
@@ -102,6 +103,16 @@
     def all_out(ref, sem):
         remote(ref, ref, sem, sem, partner).wait_send()
 
+    def along_z(body):
+        body(NZ // 2)
+
+        def step(j, c):
+            body(NZ // 2 - j)
+            body(NZ // 2 + j)
+            return c
+
+        lax.fori_loop(1, NZ // 2, step, 0)
+
     def each(n, body):
         def step(j, c):
             body(j)
@@ -117,11 +128,11 @@
     def block_device(k):
         return (lax.rem(s + (k + NX * NZ), NX * NZ), t)
 
+    along_z(lambda j: greet(zpeer(j)[1]))
     for k in NEAR:
         greet(block_device(k))
         greet(block_device(-k))
     each(NX, lambda j: greet(xpeer(j)[1]))
-    each(NZ, lambda j: greet(zpeer(j)[1]))
     each(NT, lambda j: greet(tpeer(j)[1]))
 
     loads = [
@@ -188,7 +199,7 @@
         o, dev = zpeer(j)
         remote(dexp_s.at[lax.div(o, 8)], dz_s.at[z], d_ss, d_rs, dev).start()
 
-    each(NZ, d_send)
+    along_z(d_send)
     dz_s[z] = dexp_s[lax.div(z, 8)]
 
     loads[3].wait()
@@ -295,6 +306,8 @@
     def pass_done(p):
         pair_copy(p).wait_send()
         share_copy(p, core).wait_send()
+        share_c(p, core).wait_send()
+        all_out(cs_s.at[p, pl.ds(0, NY - 1)], cs_ss.at[p])
         all_out(rs_s.at[p, pl.ds(0, NY - 1)], rs_ss.at[p])
         for q in (2 * p, 2 * p + 1):
             all_out(e1_s.at[q, pl.ds(0, NZ - 1)], e1_ss.at[q])
@@ -320,6 +333,12 @@
 
     def y_copy(p, o, dev, slot):
         return remote(ysrc_s.at[p], rs_s.at[p, slot], rs_ss.at[p], rs_rs.at[p], dev)
+
+    def c_copy(p, dev):
+        return remote(csrc_s.at[p], cs_s.at[p, chip], cs_ss.at[p], cs_rs.at[p], dev)
+
+    def share_c(p, half):
+        return remote(agc_s.at[p, half], agc_s.at[p, half], agc_ss.at[p], agc_rs.at[p], partner)
 
     def share_copy(p, half):
         return remote(ag_s.at[p, half], ag_s.at[p, half], ag_ss.at[p], ag_rs.at[p], partner)
@@ -343,26 +362,29 @@
         pair.wait_recv()
         both = pay_s[p, core] + pr_s[p]
         q1, q2 = unpack4(both[:, 256:])
-        mine = jnp.concatenate([both[:, :256], pack4(q1, q2, lane_half)], 1).astype(BF)
+        mine = jnp.concatenate([both[:, :128], pack4(q1, q2, lane_half)], 1).astype(BF)
         ysrc_s[p] = mine
         rs_s[p, chip] = mine
         each(NY, lambda j, p=p: y_copy(p, ypeer(j)[0], ypeer(j)[1], chip).start())
+        csrc_s[p] = both[:, 128:256]
+        cs_s[p, chip] = both[:, 128:256]
+        each(NY, lambda j, p=p: c_copy(p, ypeer(j)[1]).start())
         all_in(rs_s.at[p, pl.ds(0, NY - 1)], rs_rs.at[p])
         tot = jnp.sum(rs_s[p].astype(F32), axis=0)
-        q1, q2 = unpack4(tot[:, 256:])
+        q1, q2 = unpack4(tot[:, 128:])
         if p == 0:
             scale1 = jnp.ones_like(q1)
         else:
             scale1 = jnp.sqrt(q1 * (1.0 / CHANNELS) + EPS)
         spread = jnp.sqrt(q2 / (scale1 * scale1) * (1.0 / CHANNELS) + EPS)
-        proj = tot[:, :256] / (scale1 * spread)
+        per_row = 1.0 / (scale1 * spread)
+        proj = tot[:, :128] * per_row
         ag_s[p, core] = jnp.concatenate([proj, pack4(scale1, spread, lane_half)], 1).astype(BF)
         share_copy(p, core).start()
         share_copy(p, 1 - core).wait_recv()
-        agv = ag_s[p].reshape(ROWS, 384)
+        agv = ag_s[p].reshape(ROWS, 256)
         b_in = agv[:, :128]
-        c_out = agv[:, 128:256]
-        scale1, spread = unpack4(agv[:, 256:].astype(F32))
+        scale1, spread = unpack4(agv[:, 128:].astype(F32))
         if p == 1:
             f1 = gated_s[...] * (1.0 / scale1) * gain_s[...]
             out1[...] = f1
@@ -380,9 +402,14 @@
                 contrib = jnp.where(col < 64, one, two).astype(BF)
                 for nq in range(8):
                     cb_s[2 * p + half, 8 * (hp % 2) + nq] = contrib[nq * SLICE : (nq + 1) * SLICE]
-            each(NZ, lambda j, q=2 * p + half: e1_copy(q, zpeer(j), z).start())
+            along_z(lambda j, q=2 * p + half: e1_copy(q, zpeer(j), z).start())
             e1_s[2 * p + half, z] = cb_s[2 * p + half, z]
 
+        all_in(cs_s.at[p, pl.ds(0, NY - 1)], cs_rs.at[p])
+        agc_s[p, core] = (jnp.sum(cs_s[p], axis=0) * per_row).astype(BF)
+        share_c(p, core).start()
+        share_c(p, 1 - core).wait_recv()
+        c_out = agc_s[p].reshape(ROWS, NS)
         gram = dot(c_out, b_rows)
         for hp in range(PAIRS):
             cs = slice(hp * 128, hp * 128 + 128)
@@ -416,7 +443,7 @@
                 before = jnp.where(xx < x, decay * before + t_s[q, xx, :SLICE], before)
             for zz in range(NZ):
                 e3src_s[q, zz] = (pre_s[half, zz] + dp_s[zz, half : half + 1, :] * before).astype(BF)
-            each(NZ, lambda j, q=q: e3_copy(q, zpeer(j), z).start())
+            along_z(lambda j, q=q: e3_copy(q, zpeer(j), z).start())
             st_s[q, z] = e3src_s[q, z]
         for half in range(2):
             q = 2 * p + half
@@ -480,9 +507,12 @@
         vm((ROWS, COLS), F32),
         vm((2, 2, HALF, 384), F32),
         vm((2, HALF, 384), F32),
-        vm((2, HALF, 384), BF),
-        vm((2, NY, HALF, 384), BF),
-        vm((2, 2, HALF, 384), BF),
+        vm((2, HALF, 256), BF),
+        vm((2, NY, HALF, 256), BF),
+        vm((2, 2, HALF, 256), BF),
+        vm((2, HALF, 128), F32),
+        vm((2, NY, HALF, 128), F32),
+        vm((2, 2, HALF, 128), BF),
         vm((4, NZ, SLICE, 128), BF),
         vm((4, NZ, SLICE, 128), BF),
         vm((2, NZ, SLICE, 128), F32),
@@ -496,6 +526,7 @@
         dma((2, REACH + 1)), dma((2, REACH + 1)),
         dma, dma,
         dma((2,)), dma((2,)), dma((2,)), dma((2,)), dma((2,)), dma((2,)),
+        dma((2,)), dma((2,)), dma((2,)), dma((2,)),
         dma((4,)), dma((4,)), dma((4,)), dma((4,)), dma((4,)), dma((4,)),
         dma, dma,
     ]

time: 111 us -> 104 us (0.937)
  Pallas kernels: 109 us -> 102 us
    pallas_call x1, Pallas kernels: 109 us -> 102 us  [on_device(): pl.pallas_call(kernel, out_shape=(block, block), in_specs=[anyspace] * 3...]
where the time goes in v3:
time: 104 us
  Pallas kernels  102 us (98%)
  local copies, waits for them, and re-layouts  1.41 us (1%)
    pallas_call x1, Pallas kernels, on_device(): pl.pallas_call(kernel, out_shape=(block, block), in_specs=[anyspace] * 3...  102 us

profile of v3, /device:TPU:1, one launch (start us, length us, event | category | flops | bytes accessed | tf_op | source)
XLA Modules:
  0.0 104.3 jit_solution(5081212448553676694)
XLA Ops:
  0.6 102.2 %shard_map.95 = (f32[128,512]{1,0:T(8,128)S(1)}, f32[128,512]{1,0:T(8,128)S(1)}) custom-call(bf16[128,512]{1,0:T(8,128)(2,1)} %q_hbm.1, bf16[128,128]{1,0:T(8,128)(2,1)} %k_hbm.1, bf16[128,128]{1,0:T(8,128)(2,1)} %v_hbm.1, f32[8]{0:T(128)} %rates.1, s32[8,128]{1,0:T(8,128)} %bitcast.1, bf16[128,512]{1,0:T(8,128)(2,1)} %gate_hbm.1, f32[512]{0:T(512)} %gain_hbm.1, ...), custom_call_target="tpu_custom_call" | custom-call | tf_op jit(solution)/shard_map/pallas_call | solution.py:533
  102.9 0.7 copy.12
  103.6 0.7 copy.13

commit v4 on v3

--- a/solution.py
+++ b/solution.py
@@ -53,9 +53,9 @@
 
 
 def kernel(
-    q_hbm, k_hbm, v_hbm, rates, codes_hbm, gate_hbm, gain_hbm, w_hbm,
+    q_hbm, k_hbm, v_hbm, rates_hbm, codes_hbm, gate_hbm, gain_hbm, w_hbm,
     out1, out2,
-    q_s, k_s, v_s, codes_s, gate_s, gain_s, w_s,
+    rates, q_s, k_s, v_s, codes_s, gate_s, gain_s, w_s,
     sc_s, m_s, l_s, decay_s, tail_s, expell_s, silu_s,
     dexp_s, dz_s, dp_s,
     x_s, gated_s, y_s,
@@ -103,22 +103,15 @@
     def all_out(ref, sem):
         remote(ref, ref, sem, sem, partner).wait_send()
 
-    def along_z(body):
-        body(NZ // 2)
+    def each(n, body):
+        body(n // 2)
 
         def step(j, c):
-            body(NZ // 2 - j)
-            body(NZ // 2 + j)
+            body(n // 2 - j)
+            body(n // 2 + j)
             return c
 
-        lax.fori_loop(1, NZ // 2, step, 0)
-
-    def each(n, body):
-        def step(j, c):
-            body(j)
-            return c
-
-        lax.fori_loop(1, n, step, 0)
+        lax.fori_loop(1, n // 2, step, 0)
 
     barrier = pltpu.get_barrier_semaphore()
 
@@ -128,7 +121,7 @@
     def block_device(k):
         return (lax.rem(s + (k + NX * NZ), NX * NZ), t)
 
-    along_z(lambda j: greet(zpeer(j)[1]))
+    each(NZ, lambda j: greet(zpeer(j)[1]))
     for k in NEAR:
         greet(block_device(k))
         greet(block_device(-k))
@@ -142,6 +135,7 @@
                 (k_hbm, k_s.at[0]),
                 (v_hbm, v_s.at[0]),
                 (codes_hbm, codes_s),
+                (rates_hbm, rates),
                 (q_hbm, q_s),
                 (gate_hbm, gate_s),
                 (gain_hbm, gain_s.at[0]),
@@ -174,6 +168,7 @@
     lower = row >= col
     upper = jnp.where(row <= col, 1.0, 0.0).astype(BF)
     loads[2].wait()
+    loads[3].wait()
     codes = codes_s[...]
     code_hi = lax.shift_right_logical(codes, 7).astype(F32).astype(BF)
     code_lo = (codes & 127).astype(F32).astype(BF)
@@ -199,10 +194,10 @@
         o, dev = zpeer(j)
         remote(dexp_s.at[lax.div(o, 8)], dz_s.at[z], d_ss, d_rs, dev).start()
 
-    along_z(d_send)
+    each(NZ, d_send)
     dz_s[z] = dexp_s[lax.div(z, 8)]
 
-    loads[3].wait()
+    loads[4].wait()
     scale = math.log2(math.e) / math.sqrt(HS)
     diff = col - row
     own_k = k_s[0]
@@ -214,7 +209,7 @@
         l_s[h] = jnp.exp2((sc - m) * scale)
         sc_s[0, h] = sc
 
-    loads[4].wait()
+    loads[5].wait()
     g = gate_s[...].astype(F32)
     silu_s[...] = g / (1.0 + jnp.exp(-g))
 
@@ -292,8 +287,8 @@
         mixed = mixed + dot(last, v_s[REACH])
         x_s[:, h * HS : (h + 1) * HS] = mixed.astype(BF)
 
-    loads[5].wait()
     loads[6].wait()
+    loads[7].wait()
 
     def kv_done():
         for i in range(2):
@@ -402,7 +397,7 @@
                 contrib = jnp.where(col < 64, one, two).astype(BF)
                 for nq in range(8):
                     cb_s[2 * p + half, 8 * (hp % 2) + nq] = contrib[nq * SLICE : (nq + 1) * SLICE]
-            along_z(lambda j, q=2 * p + half: e1_copy(q, zpeer(j), z).start())
+            each(NZ, lambda j, q=2 * p + half: e1_copy(q, zpeer(j), z).start())
             e1_s[2 * p + half, z] = cb_s[2 * p + half, z]
 
         all_in(cs_s.at[p, pl.ds(0, NY - 1)], cs_rs.at[p])
@@ -443,7 +438,7 @@
                 before = jnp.where(xx < x, decay * before + t_s[q, xx, :SLICE], before)
             for zz in range(NZ):
                 e3src_s[q, zz] = (pre_s[half, zz] + dp_s[zz, half : half + 1, :] * before).astype(BF)
-            along_z(lambda j, q=q: e3_copy(q, zpeer(j), z).start())
+            each(NZ, lambda j, q=q: e3_copy(q, zpeer(j), z).start())
             st_s[q, z] = e3src_s[q, z]
         for half in range(2):
             q = 2 * p + half
@@ -485,6 +480,7 @@
     anyspace = pl.BlockSpec(memory_space=pl.ANY)
     block = vm((ROWS, COLS), F32)
     scratch = [
+        pltpu.SMEM((NH,), F32),
         vm((ROWS, COLS), BF),
         vm((REACH + 1, ROWS, HS), BF),
         vm((REACH + 1, ROWS, HS), BF),
@@ -522,7 +518,7 @@
         vm((4, NZ, SLICE, 128), BF),
         vm((8, 128), F32),
         vm((NT, 8, 128), F32),
-        dma((7,)),
+        dma((8,)),
         dma((2, REACH + 1)), dma((2, REACH + 1)),
         dma, dma,
         dma((2,)), dma((2,)), dma((2,)), dma((2,)), dma((2,)), dma((2,)),
@@ -533,7 +529,7 @@
     return pl.pallas_call(
         kernel,
         out_shape=(block, block),
-        in_specs=[anyspace] * 3 + [pl.BlockSpec(memory_space=pltpu.SMEM)] + [anyspace] * 4,
+        in_specs=[anyspace] * 8,
         out_specs=(pl.BlockSpec(memory_space=vm),) * 2,
         scratch_shapes=scratch,
         compiler_params=pltpu.CompilerParams(

time: 104 us -> 103 us (level)
    pallas_call x1, Pallas kernels: 102 us -> 101 us  [on_device(): pl.pallas_call(kernel, out_shape=(block, block), in_specs=[anyspace] * 8,...]
where the time goes in v4:
time: 103 us
  Pallas kernels  101 us (98%)
  local copies, waits for them, and re-layouts  1.41 us (1%)
    pallas_call x1, Pallas kernels, on_device(): pl.pallas_call(kernel, out_shape=(block, block), in_specs=[anyspace] * 8,...  101 us

profile of v4, /device:TPU:1, one launch (start us, length us, event | category | flops | bytes accessed | tf_op | source)
XLA Modules:
  0.0 102.6 jit_solution(3766296576719024923)
XLA Ops:
  0.6 100.6 %shard_map.95 = (f32[128,512]{1,0:T(8,128)S(1)}, f32[128,512]{1,0:T(8,128)S(1)}) custom-call(bf16[128,512]{1,0:T(8,128)(2,1)} %q_hbm.1, bf16[128,128]{1,0:T(8,128)(2,1)} %k_hbm.1, bf16[128,128]{1,0:T(8,128)(2,1)} %v_hbm.1, f32[8]{0:T(128)} %rates_hbm.1, s32[8,128]{1,0:T(8,128)} %bitcast.1, bf16[128,512]{1,0:T(8,128)(2,1)} %gate_hbm.1, f32[512]{0:T(512)} %gain_hbm.1, ...), custom_call_target="tpu_custom_call" | custom-call | tf_op jit(solution)/shard_map/pallas_call | solution.py:529
  101.2 0.7 copy.12
  101.9 0.7 copy.13

commit v5 on v4

--- a/solution.py
+++ b/solution.py
@@ -56,7 +56,7 @@
     q_hbm, k_hbm, v_hbm, rates_hbm, codes_hbm, gate_hbm, gain_hbm, w_hbm,
     out1, out2,
     rates, q_s, k_s, v_s, codes_s, gate_s, gain_s, w_s,
-    sc_s, m_s, l_s, decay_s, tail_s, expell_s, silu_s,
+    sc_s, p_s, m_s, l_s, decay_s, tail_s, expell_s, silu_s,
     dexp_s, dz_s, dp_s,
     x_s, gated_s, y_s,
     pay_s, pr_s, ysrc_s, rs_s, ag_s, csrc_s, cs_s, agc_s,
@@ -228,16 +228,14 @@
             for k in (a, b):
                 arrived(i, k)
                 hop(i, k, RELAY[k][0]).start()
-        for n in (1, 2):
-            for k in (a, b):
-                for i in range(2):
+            for n in (1, 2):
+                for k in (a, b):
                     for to in RELAY[k][n : n + 1]:
                         hop(i, k, to).start()
 
     def come(*slots):
         for b in slots:
             arrived(0, b)
-            arrived(1, b)
 
     def attend(a, b):
         big = jnp.int32(1 << 20)
@@ -279,13 +277,16 @@
     for h in range(HEADS):
         m = m_s[h]
         inv = 1.0 / jnp.sum(l_s[h], axis=1, keepdims=True)
-        mixed = jnp.zeros((ROWS, HS), F32)
-        for a in range(0, REACH, 2):
-            parts = [(jnp.exp2((sc_s[k, h] - m) * scale) * inv).astype(BF) for k in (a, a + 1)]
-            mixed = mixed + dot(jnp.concatenate(parts, 1), v_s[a : a + 2].reshape(2 * ROWS, HS))
-        last = (jnp.exp2((sc_s[REACH, h] - m) * scale) * inv).astype(BF)
-        mixed = mixed + dot(last, v_s[REACH])
-        x_s[:, h * HS : (h + 1) * HS] = mixed.astype(BF)
+        for k in range(REACH + 1):
+            p_s[h, :, k * ROWS : (k + 1) * ROWS] = (
+                jnp.exp2((sc_s[k, h] - m) * scale) * inv
+            ).astype(BF)
+    for k in range(1, REACH + 1):
+        if k not in RELAY:
+            arrived(1, k)
+    window_v = v_s[...].reshape((REACH + 1) * ROWS, HS)
+    for h in range(HEADS):
+        x_s[:, h * HS : (h + 1) * HS] = dot(p_s[h], window_v).astype(BF)
 
     loads[6].wait()
     loads[7].wait()
@@ -489,6 +490,7 @@
         vm((1, COLS), F32),
         vm((COLS, 256), BF),
         vm((REACH + 1, HEADS, ROWS, HS), F32),
+        vm((HEADS, ROWS, (REACH + 1) * ROWS), BF),
         vm((HEADS, ROWS, HS), F32),
         vm((HEADS, ROWS, HS), F32),
         vm((NH, ROWS, ROWS), F32),

time: 103 us -> 102 us (level)
  Pallas kernels: 101 us -> 99.5 us
    pallas_call x1, Pallas kernels: 101 us -> 99.5 us  [on_device(): pl.pallas_call(kernel, out_shape=(block, block), in_specs=[anyspace] * 8,...]
where the time goes in v5:
time: 102 us
  Pallas kernels  99.5 us (98%)
  local copies, waits for them, and re-layouts  1.41 us (1%)
    pallas_call x1, Pallas kernels, on_device(): pl.pallas_call(kernel, out_shape=(block, block), in_specs=[anyspace] * 8,...  99.5 us

profile of v5, /device:TPU:1, one launch (start us, length us, event | category | flops | bytes accessed | tf_op | source)
XLA Modules:
  0.0 101.5 jit_solution(1851223635020390484)
XLA Ops:
  0.6 99.5 %shard_map.95 = (f32[128,512]{1,0:T(8,128)S(1)}, f32[128,512]{1,0:T(8,128)S(1)}) custom-call(bf16[128,512]{1,0:T(8,128)(2,1)} %q_hbm.1, bf16[128,128]{1,0:T(8,128)(2,1)} %k_hbm.1, bf16[128,128]{1,0:T(8,128)(2,1)} %v_hbm.1, f32[8]{0:T(128)} %rates_hbm.1, s32[8,128]{1,0:T(8,128)} %bitcast.1, bf16[128,512]{1,0:T(8,128)(2,1)} %gate_hbm.1, f32[512]{0:T(512)} %gain_hbm.1, ...), custom_call_target="tpu_custom_call" | custom-call | tf_op jit(solution)/shard_map/pallas_call | solution.py:531
  100.1 0.7 copy.12
  100.8 0.7 copy.13

commit v6 on v5

--- a/solution.py
+++ b/solution.py
@@ -197,22 +197,6 @@
     each(NZ, d_send)
     dz_s[z] = dexp_s[lax.div(z, 8)]
 
-    loads[4].wait()
-    scale = math.log2(math.e) / math.sqrt(HS)
-    diff = col - row
-    own_k = k_s[0]
-    for h in range(HEADS):
-        qh = q_s[:, h * HS : (h + 1) * HS]
-        sc = jnp.where(lower, dot(qh, own_k, 1, 1), NEG)
-        m = jnp.max(sc, axis=1, keepdims=True)
-        m_s[h] = jnp.broadcast_to(m, (ROWS, HS))
-        l_s[h] = jnp.exp2((sc - m) * scale)
-        sc_s[0, h] = sc
-
-    loads[5].wait()
-    g = gate_s[...].astype(F32)
-    silu_s[...] = g / (1.0 + jnp.exp(-g))
-
     def decay_products():
         all_in(dz_s.at[pl.ds(0, NZ - 1)], d_rs)
         running = jnp.ones((2, 128), F32)
@@ -259,6 +243,23 @@
             sc_s[b, h] = sc[:, HS:]
 
     relay(3, 13)
+    loads[4].wait()
+    scale = math.log2(math.e) / math.sqrt(HS)
+    diff = col - row
+    own_k = k_s[0]
+    for h in range(HEADS):
+        qh = q_s[:, h * HS : (h + 1) * HS]
+        sc = jnp.where(lower, dot(qh, own_k, 1, 1), NEG)
+        m = jnp.max(sc, axis=1, keepdims=True)
+        m_s[h] = jnp.broadcast_to(m, (ROWS, HS))
+        l_s[h] = jnp.exp2((sc - m) * scale)
+        sc_s[0, h] = sc
+
+    loads[5].wait()
+    g = gate_s[...].astype(F32)
+    silu_s[...] = g / (1.0 + jnp.exp(-g))
+
+
     come(1, 15)
     attend(1, 15)
     attend(3, 13)
@@ -364,8 +365,8 @@
         each(NY, lambda j, p=p: y_copy(p, ypeer(j)[0], ypeer(j)[1], chip).start())
         csrc_s[p] = both[:, 128:256]
         cs_s[p, chip] = both[:, 128:256]
+        all_in(rs_s.at[p, pl.ds(0, NY - 1)], rs_rs.at[p])
         each(NY, lambda j, p=p: c_copy(p, ypeer(j)[1]).start())
-        all_in(rs_s.at[p, pl.ds(0, NY - 1)], rs_rs.at[p])
         tot = jnp.sum(rs_s[p].astype(F32), axis=0)
         q1, q2 = unpack4(tot[:, 128:])
         if p == 0:

time: 102 us -> 101 us (level)
  no operation moved by 1% of the time
where the time goes in v6:
time: 101 us
  Pallas kernels  99.1 us (98%)
  local copies, waits for them, and re-layouts  1.41 us (1%)
    pallas_call x1, Pallas kernels, on_device(): pl.pallas_call(kernel, out_shape=(block, block), in_specs=[anyspace] * 8,...  99.1 us

profile of v6, /device:TPU:1, one launch (start us, length us, event | category | flops | bytes accessed | tf_op | source)
XLA Modules:
  0.0 101.1 jit_solution(9424777799604027969)
XLA Ops:
  0.6 99.1 %shard_map.95 = (f32[128,512]{1,0:T(8,128)S(1)}, f32[128,512]{1,0:T(8,128)S(1)}) custom-call(bf16[128,512]{1,0:T(8,128)(2,1)} %q_hbm.1, bf16[128,128]{1,0:T(8,128)(2,1)} %k_hbm.1, bf16[128,128]{1,0:T(8,128)(2,1)} %v_hbm.1, f32[8]{0:T(128)} %rates_hbm.1, s32[8,128]{1,0:T(8,128)} %bitcast.1, bf16[128,512]{1,0:T(8,128)(2,1)} %gate_hbm.1, f32[512]{0:T(512)} %gain_hbm.1, ...), custom_call_target="tpu_custom_call" | custom-call | tf_op jit(solution)/shard_map/pallas_call | solution.py:532
  99.7 0.7 copy.12
  100.4 0.7 copy.13
